TPU v7x, 512 devices: a whole 4x4x16 slice. The times are simulated.
512 devices in a mesh: replica: 32 (over x, y, z_hi), fsdp: 16 (over z_lo, core).
Axes of the slice: x: 4, y: 4, z: 16 (z_hi: 2, z_lo: 8; z = z_hi * 8 + z_lo), core: 2. Of those that a mesh axis runs over, the one named last changes fastest.
Arguments:
- tokens: bfloat16 [98304, 4096], P(('replica', 'fsdp')), may hold values from -6 to 6
- grads_out: bfloat16 [98304, 1024], P(('replica', 'fsdp')), may hold values from -6 to 6
- weights: bfloat16 [32, 4096, 1024], P('replica', 'fsdp'), may hold values from -0.29882812 to 0.29882812
- moments: float32 [32, 4096, 1024], P('replica', 'fsdp'), may hold values from -6 to 6
- step: int32 [1], replicated, may hold values from 0 to 999
Outputs:
- mixed_weights: bfloat16 [32, 4096, 1024], P('replica', 'fsdp')
- new_moments: float32 [32, 4096, 1024], P('replica', 'fsdp')
All inputs are finite; a program needn't handle non-finite values.
Results may differ from a plain program's by a relative error of at most 0.001.
Values may be sent and summed in bfloat16 or wider, within the bound.
A program may use at most 64 MiB of HBM per device.

v0:
```python
from functools import partial

import jax
import jax.numpy as jnp
from jax import lax
from jax.sharding import PartitionSpec as P


def from_behind(block, axis, distance):
    devices = range(lax.axis_size(axis))
    route = [((i - distance) % len(devices), i) for i in devices]
    return lax.ppermute(block, axis, route)


def jump_by(state, reach):
    return from_behind(state, "replica", reach)


def body(tokens, grads_out, weights, moments, step):
    features = lax.all_to_all(tokens, "fsdp", split_axis=1, concat_axis=0, tiled=True)
    gradient = lax.dot_general(
        features,
        lax.all_gather(grads_out, "fsdp", axis=0, tiled=True),
        (((0,), (0,)), ((), ())),
        preferred_element_type=jnp.float32,
    )
    total_tokens = tokens.shape[0] * lax.axis_size("fsdp")
    gradient = gradient * jnp.float32(total_tokens ** (-0.5))
    new_moments = 0.9 * moments[0] + gradient
    updated = weights[0].astype(jnp.float32) - 0.05 * new_moments
    levels = lax.axis_size("replica").bit_length() - 1
    level = step[0] % levels
    branches = [partial(jump_by, reach=1 << power) for power in range(levels)]
    partner = lax.switch(level, branches, updated)
    mixed_weights = ((updated + partner) * 0.5).astype(jnp.bfloat16)
    return (mixed_weights[None], new_moments[None])


def solution(mesh):
    return jax.shard_map(
        body,
        mesh=mesh,
        in_specs=(
            P(("replica", "fsdp"), None),
            P(("replica", "fsdp"), None),
            P("replica", "fsdp", None),
            P("replica", "fsdp", None),
            P(),
        ),
        out_specs=(P("replica", "fsdp", None), P("replica", "fsdp", None)),
        check_vma=False,
    )
```

profile of v0, /device:TPU:97, one launch (start us, length us, event | category | flops | bytes accessed | tf_op | source)
XLA Modules:
  0.0 206.8 jit_solution(12496045864262289007)
XLA Ops:
  7.2 0.0 all-gather.2.cloned.1.call-start
  7.2 0.7 all-gather.2.cloned.1.call-update
  7.9 2.7 %copy.11 = bf16[24,16,8,256]{3,2,0,1:T(8,128)(2,1)} copy(bf16[24,16,8,256]{3,2,1,0:T(8,128)(2,1)} %bitcast.19) | data formatting | bytes 3145728 | tf_op jit(solution)/shard_map/all_to_all | solution.py:20
  10.6 0.0 copy-start
  10.6 12.2 %all-to-all-start = ((bf16[192,16,256]{2,0,1:T(8,128)(2,1)}), bf16[192,16,256]{2,0,1:T(8,128)(2,1)S(1)}, u32[]{:S(2)}, u32[]{:S(2)}) async-start(bf16[192,16,256]{2,0,1:T(8,128)(2,1)} %bitcast.17), calls=%async_computation | async-start | bytes 3145728 | tf_op jit(solution)/shard_map/all_to_all | solution.py:20
  23.5 97.5 %all-to-all-done = bf16[192,16,256]{2,0,1:T(8,128)(2,1)S(1)} async-done(((bf16[192,16,256]{2,0,1:T(8,128)(2,1)}), bf16[192,16,256]{2,0,1:T(8,128)(2,1)S(1)}, u32[]{:S(2)}, u32[]{:S(2)}) %all-to-all-start) | async-done | bytes 1572896 | tf_op jit(solution)/shard_map/all_to_all | solution.py:20
  120.9 41.8 %all-gather.2.cloned.1.call-done = bf16[3072,1024]{1,0:T(8,128)(2,1)} async-done(((bf16[192,1024]{1,0:T(8,128)(2,1)}), bf16[3072,1024]{1,0:T(8,128)(2,1)}) %all-gather.2.cloned.1.call-update) | async-done | bytes 6291472 | tf_op jit(solution)/shard_map/all_gather | solution.py:23
  162.7 0.0 copy-done
  162.7 5.9 %convert_subtract_fusion = (f32[256,1024]{1,0:T(8,128)S(1)}, f32[256,1024]{1,0:T(8,128)}) fusion(bf16[1,256,1024]{2,1,0:T(8,128)(2,1)S(1)} %copy-done, bf16[3072,256]{1,0:T(8,128)(2,1)S(1)} %bitcast.18, bf16[3072,1024]{1,0:T(8,128)(2,1)} %all-gather.2.cloned.1.call-done, f32[1,256,1024]{2,1,0:T(8,128)} %param.13), kind=kOutput, calls=%fused_computation.3 | convolution fusion | flops 1612185600 | bytes 11534336 | tf_op jit(solution)/shard_map/dot_general | solution.py:21
  168.6 29.1 %conditional.1 = (f32[256,1024]{1,0:T(8,128)}) conditional(s32[]{:T(128)} %clamp.3, f32[256,1024]{1,0:T(8,128)S(1)} %get-tuple-element.13, f32[256,1024]{1,0:T(8,128)S(1)} %get-tuple-element.13, f32[256,1024]{1,0:T(8,128)S(1)} %get-tuple-element.13, f32[256,1024]{1,0:T(8,128)S(1)} %get-tuple-element.13, ...), branch_computations={%region_0.1_spmd, %region_1.2_spmd, %region_2.3_spmd, %region_3.4_... | conditional | bytes 4194352 | solution.py:34
  168.6 5.0 %collective-permute-start.2 = (f32[256,1024]{1,0:T(8,128)S(1)}, f32[256,1024]{1,0:T(8,128)}, u32[]{:S(2)}, u32[]{:S(2)}) collective-permute-start(f32[256,1024]{1,0:T(8,128)S(1)} %param.2), channel_id=1, source_target_pairs={{448,0},{464,16},{480,32},{496,48},{0,64},{16,80},{32,96},{48,112}... | collective-permute-start | bytes 3145736 | tf_op jit(solution)/shard_map/cond/branch_2_fun/ppermute | solution.py:12
  173.7 24.0 %collective-permute-done.2 = f32[256,1024]{1,0:T(8,128)} collective-permute-done((f32[256,1024]{1,0:T(8,128)S(1)}, f32[256,1024]{1,0:T(8,128)}, u32[]{:S(2)}, u32[]{:S(2)}) %collective-permute-start.2) | collective-permute-done | bytes 1048608 | tf_op jit(solution)/shard_map/cond/branch_2_fun/ppermute | solution.py:12
  197.7 2.2 %fusion.1 = bf16[1,256,1024]{2,1,0:T(8,128)(2,1)} fusion(f32[256,1024]{1,0:T(8,128)S(1)} %get-tuple-element.13, f32[256,1024]{1,0:T(8,128)} %get-tuple-element.15), kind=kLoop, calls=%fused_computation.5 | loop fusion | flops 786432 | bytes 2621440 | tf_op jit(solution)/shard_map/broadcast_in_dim | solution.py:36
Async XLA Ops:
  7.2 155.6 %all-gather.2.cloned.1.call-start = ((), (), s32[]{:S(2)}) async-start(), calls=%async_computation.1 | async-start | bytes 6684672 | tf_op jit(solution)/shard_map/all_gather | solution.py:23
  10.6 152.1 %copy-start = (bf16[1,256,1024]{2,1,0:T(8,128)(2,1)S(1)}, bf16[1,256,1024]{2,1,0:T(8,128)(2,1)}, u32[]{:S(2)}) copy-start(bf16[1,256,1024]{2,1,0:T(8,128)(2,1)} %param.12) | copy-start | bytes 1572868
  10.6 110.3 %all-to-all-start = ((bf16[192,16,256]{2,0,1:T(8,128)(2,1)}), bf16[192,16,256]{2,0,1:T(8,128)(2,1)S(1)}, u32[]{:S(2)}, u32[]{:S(2)}) async-start(bf16[192,16,256]{2,0,1:T(8,128)(2,1)} %bitcast.17), calls=%async_computation | async-start | bytes 3145728 | tf_op jit(solution)/shard_map/all_to_all | solution.py:20
  168.6 29.1 %collective-permute-start.2 = (f32[256,1024]{1,0:T(8,128)S(1)}, f32[256,1024]{1,0:T(8,128)}, u32[]{:S(2)}, u32[]{:S(2)}) collective-permute-start(f32[256,1024]{1,0:T(8,128)S(1)} %param.2), channel_id=1, source_target_pairs={{448,0},{464,16},{480,32},{496,48},{0,64},{16,80},{32,96},{48,112}... | collective-permute-start | bytes 3145736 | tf_op jit(solution)/shard_map/cond/branch_2_fun/ppermute | solution.py:12
Sparse Core Ops, SparseCore 0:
  10.1 152.5 all-gather.1
where the time goes:
time: 207 us
  waiting for transfers between devices  164 us (79%)
  starting transfers between devices  17.3 us (8%)
  between operations  14.7 us (7%)
  matrix products  5.92 us (3%)
  local copies, waits for them, and re-layouts  2.72 us (1%)
  other arithmetic  2.23 us (1%)
    all_to_all x1, waiting for transfers between devices, body(): lax.all_to_all(tokens, 'fsdp', split_axis=1, concat_axis=0, tiled=True)  97.5 us
    all_gather x1, waiting for transfers between devices, body(): lax.all_gather(grads_out, 'fsdp', axis=0, tiled=True)  41.8 us
    ppermute x1, waiting for transfers between devices, from_behind(): return lax.ppermute(block, axis, route)  24 us
    all_to_all x1, starting transfers between devices, body(): lax.all_to_all(tokens, 'fsdp', split_axis=1, concat_axis=0, tiled=True)  12.2 us
    dot_general x1, matrix products, body(): lax.dot_general(features, lax.all_gather(grads_out, 'fsdp', axis=0, tiled...  5.92 us
    ppermute x1, starting transfers between devices, from_behind(): return lax.ppermute(block, axis, route)  5.04 us
  transfers between devices with their start and end apart: 3, of which 3 were waited for; matrix products, arithmetic and copies ran while one was open for 1% of the time, Pallas kernels for 0%

commit v1 on v0

v1 whole, which is shorter than its diff:
```python
import functools

import jax
import jax.numpy as jnp
from jax import lax
from jax.experimental import pallas as pl
from jax.experimental.pallas import tpu as pltpu
from jax.sharding import PartitionSpec as P

MESH = pl.DeviceIdType.MESH
TOP = 32767.0
TINY = 1e-30
UNITS = 4
HOP = 2
LANES = 256


def kernel(
    replicas,
    chips,
    distance,
    scale,
    tokens_hbm,
    grads_hbm,
    weights_hbm,
    moments_hbm,
    mixed_hbm,
    new_hbm,
    tok,
    grad,
    buf,
    factor,
    part,
    weights,
    moments,
    new,
    updated,
    mixed,
    out_buf,
    out_factor,
    in_buf,
    in_factor,
    own_sem,
    sib_send,
    sib_recv,
    load_sem,
    send,
    recv,
    factor_send,
    factor_recv,
    gossip_send,
    gossip_recv,
    gossip_factor_send,
    gossip_factor_recv,
    new_sem,
    mixed_sem,
):
    last = chips - 1
    features, columns = updated.shape
    rows = features // UNITS
    width = min(LANES, columns)
    replica = lax.axis_index("replica")
    me = lax.axis_index("fsdp")
    chip = me // 2
    core = me % 2
    sibling = chip * 2 + 1 - core
    left = jnp.maximum(me - 2, 0)
    right = jnp.minimum(me + 2, 2 * chips - 1)
    partner = (replica + distance) % replicas
    source = (replica + replicas - distance) % replicas

    def piece(target, which):
        start = pl.multiple_of((2 * target + which) * features, features)
        return tokens_hbm.at[:, pl.ds(start, features)]

    def own_copy(target):
        return pltpu.make_async_copy(
            piece(target, core), tok.at[target, core], own_sem.at[target]
        )

    def sibling_copy(target):
        return pltpu.make_async_remote_copy(
            src_ref=piece(target, 1 - core),
            dst_ref=tok.at[target, core],
            send_sem=sib_send.at[target],
            recv_sem=sib_recv.at[target],
            device_id={"fsdp": sibling},
            device_id_type=MESH,
        )

    own_grad = pltpu.make_async_copy(grads_hbm, grad.at[core], own_sem.at[chips])
    sibling_grad = pltpu.make_async_remote_copy(
        src_ref=grads_hbm,
        dst_ref=grad.at[core],
        send_sem=sib_send.at[chips],
        recv_sem=sib_recv.at[chips],
        device_id={"fsdp": sibling},
        device_id_type=MESH,
    )
    load_weights = pltpu.make_async_copy(weights_hbm.at[0], weights, load_sem.at[0])
    load_moments = pltpu.make_async_copy(moments_hbm.at[0], moments, load_sem.at[1])

    order = []
    for near in range(chips // 2):
        order += [near, last - near]

    barrier = pltpu.get_barrier_semaphore()
    pl.semaphore_signal(barrier, inc=1, device_id={"fsdp": sibling}, device_id_type=MESH)
    pl.semaphore_signal(barrier, inc=1, device_id={"replica": source}, device_id_type=MESH)

    @pl.when(chip > 0)
    def _():
        pl.semaphore_signal(barrier, inc=1, device_id={"fsdp": left}, device_id_type=MESH)

    @pl.when(chip < last)
    def _():
        pl.semaphore_signal(barrier, inc=1, device_id={"fsdp": right}, device_id_type=MESH)

    own_grad.start()
    for target in order:
        own_copy(target).start()
    load_weights.start()
    load_moments.start()

    pl.semaphore_wait(
        barrier, 2 + (chip > 0).astype(jnp.int32) + (chip < last).astype(jnp.int32)
    )

    sibling_grad.start()
    for target in order:
        sibling_copy(target).start()
    own_grad.wait()
    sibling_grad.wait_recv()

    def multiply(target, slot):
        own_copy(target).wait()
        sibling_copy(target).wait_recv()
        left_side = tok[target].reshape(-1, features)
        right_side = grad[...].reshape(-1, columns)
        part[slot] = lax.dot_general(
            left_side,
            right_side,
            (((0,), (0,)), ((), ())),
            preferred_element_type=jnp.float32,
        )

    def hop(way, unit):
        to = left if way == 0 else right
        data = pltpu.make_async_remote_copy(
            src_ref=buf.at[way, unit],
            dst_ref=buf.at[way, unit],
            send_sem=send.at[way, unit],
            recv_sem=recv.at[way, unit],
            device_id={"fsdp": to},
            device_id_type=MESH,
        )
        factors = pltpu.make_async_remote_copy(
            src_ref=factor.at[way, unit],
            dst_ref=factor.at[way, unit],
            send_sem=factor_send.at[way, unit],
            recv_sem=factor_recv.at[way, unit],
            device_id={"fsdp": to},
            device_id_type=MESH,
        )
        return data, factors

    def gossip(unit):
        data = pltpu.make_async_remote_copy(
            src_ref=out_buf.at[unit],
            dst_ref=in_buf.at[unit],
            send_sem=gossip_send.at[unit],
            recv_sem=gossip_recv.at[unit],
            device_id={"replica": partner},
            device_id_type=MESH,
        )
        factors = pltpu.make_async_remote_copy(
            src_ref=out_factor.at[unit],
            dst_ref=in_factor.at[unit],
            send_sem=gossip_factor_send.at[unit],
            recv_sem=gossip_factor_recv.at[unit],
            device_id={"replica": partner},
            device_id_type=MESH,
        )
        return data, factors

    def new_copy(unit):
        at = pl.ds(pl.multiple_of(unit * rows, rows), rows)
        return pltpu.make_async_copy(new.at[at], new_hbm.at[0, at], new_sem.at[unit])

    def mixed_copy(unit):
        at = pl.ds(pl.multiple_of(unit * rows, rows), rows)
        return pltpu.make_async_copy(mixed.at[at], mixed_hbm.at[0, at], mixed_sem.at[unit])

    def decode(data, factors):
        return data.astype(jnp.int32).astype(jnp.float32) * factors

    def encode(value):
        largest = jnp.max(jnp.abs(value), axis=0, keepdims=True)
        largest = jnp.maximum(largest, TINY)
        code = jnp.round(value * (TOP / largest * (1.0 - 1e-6)))
        return code.astype(jnp.int32).astype(jnp.int16), largest * (1.0 / TOP / (1.0 - 1e-6))

    def forward(way, unit, target, has_upstream):
        index = unit % UNITS

        @pl.when(index == 0)
        def _():
            multiply(target, way)

        @pl.when(has_upstream)
        def _():
            for copy in hop(way, unit):
                copy.wait_recv()

        at = pl.ds(pl.multiple_of(index * rows, rows), rows)

        @pl.when(has_upstream)
        def _():
            for begin in range(0, columns, width):
                cut = slice(begin, begin + width)
                value = part[way, at, cut] + decode(buf[way, unit, :, cut], factor[way, unit, :, cut])
                buf[way, unit, :, cut], factor[way, unit, :, cut] = encode(value)

        @pl.when(jnp.logical_not(has_upstream))
        def _():
            for begin in range(0, columns, width):
                cut = slice(begin, begin + width)
                buf[way, unit, :, cut], factor[way, unit, :, cut] = encode(part[way, at, cut])

        for copy in hop(way, unit):
            copy.start()

    from_right = chip * UNITS
    from_left = (last - chip) * UNITS
    lag_right = (last - chip) * HOP
    lag_left = chip * HOP

    def finish(unit):
        @pl.when(unit == 0)
        def _():
            multiply(chip, 2)
            load_weights.wait()
            load_moments.wait()

        at = pl.ds(pl.multiple_of(unit * rows, rows), rows)

        for way, begin_unit, there in ((0, from_right, chip < last), (1, from_left, chip > 0)):

            @pl.when(there)
            def _(way=way, begin_unit=begin_unit):
                arrived = jnp.minimum(begin_unit, last * UNITS - UNITS) + unit
                for copy in hop(way, arrived):
                    copy.wait_recv()
                for begin in range(0, columns, width):
                    cut = slice(begin, begin + width)
                    part[2, at, cut] += decode(
                        buf[way, arrived, :, cut], factor[way, arrived, :, cut]
                    )

        for begin in range(0, columns, width):
            cut = slice(begin, begin + width)
            moment = 0.9 * moments[at, cut] + part[2, at, cut] * scale
            new[at, cut] = moment
            value = weights[at, cut].astype(jnp.float32) - 0.05 * moment
            updated[at, cut] = value
            out_buf[unit, :, cut], out_factor[unit, :, cut] = encode(value)
        for copy in gossip(unit):
            copy.start()
        new_copy(unit).start()

    begin_finish = jnp.maximum(
        jnp.where(chip < last, from_right + lag_right, 0),
        jnp.where(chip > 0, from_left + lag_left, 0),
    )

    def step(i, carry):
        unit_l = i - lag_right
        unit_r = i - lag_left
        unit_o = i - begin_finish

        @pl.when(jnp.logical_and(unit_l >= 0, unit_l < from_right))
        def _():
            forward(0, unit_l, unit_l // UNITS, chip < last)

        @pl.when(jnp.logical_and(unit_r >= 0, unit_r < from_left))
        def _():
            forward(1, unit_r, last - unit_r // UNITS, chip > 0)

        @pl.when(jnp.logical_and(unit_o >= 0, unit_o < UNITS))
        def _():
            finish(unit_o)

        return carry

    steps = last * max(UNITS, HOP) + UNITS + HOP
    lax.fori_loop(0, steps, step, 0)

    def mix(unit, carry):
        for copy in gossip(unit):
            copy.wait_recv()
        at = pl.ds(pl.multiple_of(unit * rows, rows), rows)
        for begin in range(0, columns, width):
            cut = slice(begin, begin + width)
            theirs = decode(in_buf[unit, :, cut], in_factor[unit, :, cut])
            mixed[at, cut] = ((updated[at, cut] + theirs) * 0.5).astype(jnp.bfloat16)
        mixed_copy(unit).start()
        return carry

    lax.fori_loop(0, UNITS, mix, 0)

    def drain_left(unit, carry):
        for copy in hop(0, unit):
            copy.wait_send()
        return carry

    def drain_right(unit, carry):
        for copy in hop(1, unit):
            copy.wait_send()
        return carry

    lax.fori_loop(0, from_right, drain_left, 0)
    lax.fori_loop(0, from_left, drain_right, 0)
    sibling_grad.wait_send()
    for target in range(chips):
        sibling_copy(target).wait_send()

    def drain(unit, carry):
        for copy in gossip(unit):
            copy.wait_send()
        new_copy(unit).wait()
        mixed_copy(unit).wait()
        return carry

    lax.fori_loop(0, UNITS, drain, 0)


def step_with(level, replicas, members, tokens, grads_out, weights, moments):
    chips = members // 2
    held, features_all = tokens.shape
    columns = grads_out.shape[1]
    features = weights.shape[1]
    rows = features // UNITS
    passed = (chips - 1) * UNITS
    dma = pltpu.SemaphoreType.DMA
    return pl.pallas_call(
        functools.partial(
            kernel, replicas, chips, 1 << level, float((held * members) ** -0.5)
        ),
        out_shape=(
            jax.ShapeDtypeStruct(weights.shape, jnp.bfloat16),
            jax.ShapeDtypeStruct(moments.shape, jnp.float32),
        ),
        in_specs=[pl.BlockSpec(memory_space=pl.ANY)] * 4,
        out_specs=[pl.BlockSpec(memory_space=pl.ANY)] * 2,
        scratch_shapes=[
            pltpu.VMEM((chips, 2, held, features), jnp.bfloat16),
            pltpu.VMEM((2, held, columns), jnp.bfloat16),
            pltpu.VMEM((2, passed, rows, columns), jnp.int16),
            pltpu.VMEM((2, passed, 1, columns), jnp.float32),
            pltpu.VMEM((3, features, columns), jnp.float32),
            pltpu.VMEM((features, columns), jnp.bfloat16),
            pltpu.VMEM((features, columns), jnp.float32),
            pltpu.VMEM((features, columns), jnp.float32),
            pltpu.VMEM((features, columns), jnp.float32),
            pltpu.VMEM((features, columns), jnp.bfloat16),
            pltpu.VMEM((UNITS, rows, columns), jnp.int16),
            pltpu.VMEM((UNITS, 1, columns), jnp.float32),
            pltpu.VMEM((UNITS, rows, columns), jnp.int16),
            pltpu.VMEM((UNITS, 1, columns), jnp.float32),
            dma((chips + 1,)),
            dma((chips + 1,)),
            dma((chips + 1,)),
            dma((2,)),
            dma((2, passed)),
            dma((2, passed)),
            dma((2, passed)),
            dma((2, passed)),
            dma((UNITS,)),
            dma((UNITS,)),
            dma((UNITS,)),
            dma((UNITS,)),
            dma((UNITS,)),
            dma((UNITS,)),
        ],
        compiler_params=pltpu.CompilerParams(
            collective_id=level, has_side_effects=True, vmem_limit_bytes=44 * 1024 * 1024
        ),
        cost_estimate=pl.CostEstimate(
            flops=2 * held * members * features * columns,
            bytes_accessed=2 * tokens.size + 10 * features * columns,
            transcendentals=0,
        ),
    )(tokens, grads_out, weights, moments)


def solution(mesh):
    replicas, members = mesh.shape["replica"], mesh.shape["fsdp"]
    levels = replicas.bit_length() - 1

    def body(tokens, grads_out, weights, moments, step):
        level = step[0] % levels
        branches = [
            functools.partial(step_with, power, replicas, members) for power in range(levels)
        ]
        return lax.switch(level, branches, tokens, grads_out, weights, moments)

    return jax.shard_map(
        body,
        mesh=mesh,
        in_specs=(
            P(("replica", "fsdp"), None),
            P(("replica", "fsdp"), None),
            P("replica", "fsdp", None),
            P("replica", "fsdp", None),
            P(),
        ),
        out_specs=(P("replica", "fsdp", None), P("replica", "fsdp", None)),
        check_vma=False,
    )
```

time: 207 us -> 103 us (0.50)
  the two profiles are of different devices: /device:TPU:97 before, /device:TPU:33 now
where the time goes in v1:
time: 103 us
  Pallas kernels  100 us (97%)
  local copies, waits for them, and re-layouts  1.77 us (2%)
  between operations  1.3 us (1%)
    pallas_call x1, Pallas kernels, step_with(): pl.pallas_call(functools.partial(kernel, replicas, chips, 1 << level, flo...  100 us

profile of v1, /device:TPU:33, one launch (start us, length us, event | category | flops | bytes accessed | tf_op | source)
XLA Modules:
  0.0 103.1 jit_solution(3661368357083530759)
XLA Ops:
  1.3 100.0 %conditional.1 = ((bf16[1,256,1024]{2,1,0:T(8,128)(2,1)S(1)}, f32[1,256,1024]{2,1,0:T(8,128)S(1)})) conditional(s32[]{:T(128)} %clamp.3, (bf16[192,4096]{1,0:T(8,128)(2,1)}, bf16[192,1024]{1,0:T(8,128)(2,1)}, bf16[1,256,1024]{2,1,0:T(8,128)(2,1)}, f32[1,256,1024]{2,1,0:T(8,128)}) %tuple.22, ...), branch_computations={%region_0.1_spmd, %region_1.2_spmd, %region_2.3_spmd, %region_3.4_... | conditional | flops 1610612736 | bytes 4194312 | solution.py:405
  1.3 100.0 %branch_4_fun.1 = (bf16[1,256,1024]{2,1,0:T(8,128)(2,1)S(1)}, f32[1,256,1024]{2,1,0:T(8,128)S(1)}) custom-call(bf16[192,4096]{1,0:T(8,128)(2,1)} %get-tuple-element.56.tokens_hbm, bf16[192,1024]{1,0:T(8,128)(2,1)} %get-tuple-element.57.grads_hbm, bf16[1,256,1024]{2,1,0:T(8,128)(2,1)} %get-tuple-element.58.weights_hbm, ...), custom_call_target="tpu_custom_call" | custom-call | flops 1610612736 | bytes 4194304 | tf_op jit(solution)/shard_map/cond/branch_4_fun/pallas_call | solution.py:345
  101.3 0.8 copy.30
  102.1 1.0 copy.31
